TPU v7x, 32 devices: a whole 2x2x4 slice. The times are simulated.
32 devices in a mesh: pts: 8 (over y, x, core), lists: 4 (over z).
Axes of the slice: x: 2, y: 2, z: 4, core: 2. Of those that a mesh axis runs over, the one named last changes fastest.
Arguments:
- points: bfloat16 [3072, 256], P('pts'), may hold values from -4 to 4
- centroids: bfloat16 [16384, 256], P('lists'), may hold values from -0.375 to 0.375
- prior: int32 [3072], P('pts'), may hold values from 0 to 16383
- loads: int32 [16384], P('lists'), may hold values from 2 to 14, as said below
Outputs:
- centroid_means: float32 [256, 16384], P('pts', 'lists')
- log_col_scale: float32 [16384], P('lists')
Inputs may be any that keep to these rules, and one draw needn't show every extreme that they name: Lists 2k and 2k + 1 have loads 8 + e and 8 - e for some e of 0 to 6, so all loads sum to 131072.
All inputs are finite; a program needn't handle non-finite values.
Results may differ from a plain program's by a relative error of at most 0.003.
Values sent between devices are 32-bit elements; how exact they have to be, the bound alone decides.
A program may use at most 64 MiB of HBM per device.

v0:
```python
import jax
import jax.numpy as jnp
from jax import lax
from jax.sharding import PartitionSpec as P

ITERS = 3
BLOCK = 512


def kernel_tile(points, cent_block, prior, start):
    score = lax.dot_general(
        points, cent_block, (((1,), (1,)), ((), ())), preferred_element_type=jnp.float32
    )
    cols = start + lax.iota(jnp.int32, cent_block.shape[0])
    hit = (prior[:, None] == cols[None, :]).astype(jnp.float32)
    return jnp.exp(3.0 * score + 10.0 * hit)


def point_mass(partial_value):
    return lax.psum(partial_value, "lists")


def list_mass(partial_value):
    return lax.psum(partial_value, "pts")


def local(points, centroids, prior, loads):
    n_lists = centroids.shape[0]
    count = n_lists // BLOCK
    offset = lax.axis_index("lists") * n_lists
    total_pts = points.shape[0] * lax.axis_size("pts")
    total_lists = n_lists * lax.axis_size("lists")
    target = loads.astype(jnp.float32) * (total_pts / (8.0 * total_lists))

    def tile(index):
        block = centroids[index * BLOCK : (index + 1) * BLOCK]
        return kernel_tile(points, block, prior, offset + index * BLOCK)

    col_scale = jnp.ones((n_lists,), jnp.float32)
    row_scale = jnp.ones((points.shape[0],), jnp.float32)
    for step in range(ITERS):
        partial_value = jnp.zeros((points.shape[0],), jnp.float32)
        for index in range(count):
            partial_value = partial_value + jnp.sum(
                tile(index) * col_scale[None, index * BLOCK : (index + 1) * BLOCK], axis=1
            )
        row_scale = 1.0 / point_mass(partial_value)
        pieces = [jnp.sum(tile(index) * row_scale[:, None], axis=0) for index in range(count)]
        col_scale = target / list_mass(jnp.concatenate(pieces))
    plan = jnp.concatenate(
        [
            (
                tile(index)
                * row_scale[:, None]
                * col_scale[None, index * BLOCK : (index + 1) * BLOCK]
            ).astype(jnp.bfloat16)
            for index in range(count)
        ],
        axis=1,
    )
    sums = lax.psum_scatter(
        lax.dot_general(points, plan, (((0,), (0,)), ((), ())), preferred_element_type=jnp.float32),
        "pts",
        scatter_dimension=0,
        tiled=True,
    )
    return (sums / target[None, :], jnp.log(col_scale))


def solution(mesh):
    return jax.shard_map(
        local,
        mesh=mesh,
        in_specs=(P("pts", None), P("lists", None), P("pts"), P("lists")),
        out_specs=(P("pts", "lists"), P("lists")),
        check_vma=False,
    )
```

profile of v0, /device:TPU:0, one launch (start us, length us, event | category | flops | bytes accessed | tf_op | source)
XLA Modules:
  0.0 205.6 jit_solution(14971672180922664066)
XLA Ops:
  8.1 1.4 fusion.40
  9.5 1.4 fusion.41
  13.0 1.2 fusion.45
  15.5 1.2 fusion.46
  16.7 13.5 %psum.42 = f32[384]{0:T(512)S(1)} all-reduce(f32[384]{0:T(512)S(1)} %add_add_fusion.2), channel_id=1, replica_groups=mesh['pts'=8,'lists'=4] {'lists'}, use_global_device_ids=true, to_apply=%region_8.0 | all-reduce | flops 384 | bytes 3072 | tf_op jit(solution)/shard_map/psum | solution.py:20
  30.2 2.7 %multiply_reduce_fusion.24 = (f32[512]{0:T(512)S(1)}, f32[512]{0:T(512)S(1)}, f32[512]{0:T(512)S(1)}, f32[512]{0:T(512)S(1)}, f32[512]{0:T(512)S(1)}, /*index=5*/f32[512]{0:T(512)S(1)}, f32[512]{0:T(512)S(1)}, f32[512]{0:T(512)S(1)}) fusion(f32[384,512]{1,0:T(8,128)S(1)} %get-tuple-element.59, f32[384]{0:T(512)S(1)} %broadcast_divide_fusion.3, ...), kind=kLoop, calls=%fused_computation.58 | loop fusion | flops 3141632 | bytes 6309376 | tf_op jit(solution)/shard_map/reduce_sum | solution.py:48
  33.0 22.3 %psum.43 = f32[4096]{0:T(1024)S(1)} all-reduce(f32[4096]{0:T(1024)S(1)} %constant_dynamic-update-slice_fusion.3), channel_id=1, replica_groups=mesh['pts'=8,'lists'=4] {'pts'}, use_global_device_ids=true, to_apply=%region_17.0 | all-reduce | flops 4096 | bytes 32768 | tf_op jit(solution)/shard_map/psum | solution.py:24
  55.4 1.7 multiply_reduce_fusion.22
  57.7 8.4 %psum.44 = f32[384]{0:T(512)S(1)} all-reduce(f32[384]{0:T(512)S(1)} %add_add_fusion.1), channel_id=1, replica_groups=mesh['pts'=8,'lists'=4] {'lists'}, use_global_device_ids=true, to_apply=%region_26.0 | all-reduce | flops 384 | bytes 3072 | tf_op jit(solution)/shard_map/psum | solution.py:20
  66.1 2.7 %multiply_reduce_fusion.8 = (f32[512]{0:T(512)S(1)}, f32[512]{0:T(512)S(1)}, f32[512]{0:T(512)S(1)}, f32[512]{0:T(512)S(1)}, f32[512]{0:T(512)S(1)}, /*index=5*/f32[512]{0:T(512)S(1)}, f32[512]{0:T(512)S(1)}, f32[512]{0:T(512)S(1)}) fusion(f32[384,512]{1,0:T(8,128)S(1)} %get-tuple-element.59, f32[384]{0:T(512)S(1)} %broadcast_divide_fusion.2, ...), kind=kLoop, calls=%fused_computation.42 | loop fusion | flops 3141632 | bytes 6309376 | tf_op jit(solution)/shard_map/reduce_sum | solution.py:48
  68.9 22.4 %psum.45 = f32[4096]{0:T(1024)S(1)} all-reduce(f32[4096]{0:T(1024)S(1)} %constant_dynamic-update-slice_fusion.4), channel_id=1, replica_groups=mesh['pts'=8,'lists'=4] {'pts'}, use_global_device_ids=true, to_apply=%region_35.0 | all-reduce | flops 4096 | bytes 32768 | tf_op jit(solution)/shard_map/psum | solution.py:24
  91.3 1.4 multiply_reduce_fusion.6
  93.8 10.4 %psum.46 = f32[384]{0:T(512)S(1)} all-reduce(f32[384]{0:T(512)S(1)} %add_add_fusion), channel_id=1, replica_groups=mesh['pts'=8,'lists'=4] {'lists'}, use_global_device_ids=true, to_apply=%region_44.0 | all-reduce | flops 384 | bytes 3072 | tf_op jit(solution)/shard_map/psum | solution.py:20
  104.2 2.7 %multiply_reduce_fusion.32 = (f32[512]{0:T(512)S(1)}, f32[512]{0:T(512)S(1)}, f32[512]{0:T(512)S(1)}, f32[512]{0:T(512)S(1)}, f32[512]{0:T(512)S(1)}, /*index=5*/f32[512]{0:T(512)S(1)}, f32[512]{0:T(512)S(1)}, f32[512]{0:T(512)S(1)}) fusion(f32[384,512]{1,0:T(8,128)S(1)} %get-tuple-element.59, f32[384]{0:T(512)S(1)} %broadcast_divide_fusion.1, ...), kind=kLoop, calls=%fused_computation.66 | loop fusion | flops 3141632 | bytes 6309376 | tf_op jit(solution)/shard_map/reduce_sum | solution.py:48
  107.0 22.5 %psum.47 = f32[4096]{0:T(1024)S(1)} all-reduce(f32[4096]{0:T(1024)S(1)} %constant_dynamic-update-slice_fusion.5), channel_id=1, replica_groups=mesh['pts'=8,'lists'=4] {'pts'}, use_global_device_ids=true, to_apply=%region_53.0 | all-reduce | flops 4096 | bytes 32768 | tf_op jit(solution)/shard_map/psum | solution.py:24
  130.2 1.3 fusion.16
  131.4 1.3 fusion.17
  132.7 1.3 fusion.18
  134.7 3.3 %convolution_bitcast_fusion = f32[256,4096]{0,1:T(8,128)} fusion(bf16[384,4096]{1,0:T(8,128)(2,1)S(1)} %fusion.23, bf16[384,256]{1,0:T(8,128)(2,1)S(1)} %copy-done), kind=kOutput, calls=%fused_computation | convolution fusion | flops 805306368 | bytes 7536640 | tf_op jit(solution)/shard_map/dot_general | solution.py:62
  138.0 5.6 %copy.8 = f32[256,4096]{1,0:T(8,128)} copy(f32[256,4096]{0,1:T(8,128)} %convolution_bitcast_fusion) | data formatting | bytes 8388608
  143.6 48.8 %reduce-scatter.4.cloned.1.call-done = f32[32,4096]{1,0:T(8,128)} async-done(((f32[256,4096]{1,0:T(8,128)}), f32[32,4096]{1,0:T(8,128)}) %reduce-scatter.4.cloned.1.call-update) | async-done | bytes 524304
  192.4 1.6 copy.9
  194.0 1.8 broadcast_divide_fusion
  195.8 3.0 %copy.7 = f32[32,4096]{1,0:T(8,128)} copy(f32[32,4096]{0,1:T(8,128)} %broadcast_divide_fusion) | data formatting | bytes 1048576
  (88 shorter events, 7.3 us)
Async XLA Ops:
  7.2 0.9 copy-start
  7.2 3.7 %copy-start.9 = (s32[384]{0:T(512)S(1)}, s32[384]{0:T(512)}, u32[]{:S(2)}) copy-start(s32[384]{0:T(512)} %param.6) | copy-start | bytes 4612
  7.2 185.2 %reduce-scatter.4.cloned.1.call-start = ((), (), s32[]{:S(2)}) async-start(), calls=%async_computation.1 | async-start | bytes 4718592
  7.3 3.6 %copy-start.8 = (bf16[4096,256]{1,0:T(8,128)(2,1)S(1)}, bf16[4096,256]{1,0:T(8,128)(2,1)}, u32[]{:S(2)}) copy-start(bf16[4096,256]{1,0:T(8,128)(2,1)} %param.5) | copy-start | bytes 6291460
  30.2 25.2 %copy-start.7 = (s32[4096]{0:T(1024)S(1)}, s32[4096]{0:T(1024)}, u32[]{:S(2)}) copy-start(s32[4096]{0:T(1024)} %param.7) | copy-start | bytes 49156
  55.4 2.1 %copy-start.1 = (f32[384,512]{1,0:T(8,128)S(1)}, f32[384,512]{1,0:T(8,128)}, u32[]{:S(2)}) copy-start(f32[384,512]{1,0:T(8,128)} %get-tuple-element.67) | copy-start | bytes 2359300
  55.4 2.1 %copy-start.4 = (f32[384,512]{1,0:T(8,128)S(1)}, f32[384,512]{1,0:T(8,128)}, u32[]{:S(2)}) copy-start(f32[384,512]{1,0:T(8,128)} %get-tuple-element.69) | copy-start | bytes 2359300
  91.2 2.1 %copy-start.2 = (f32[384,512]{1,0:T(8,128)S(1)}, f32[384,512]{1,0:T(8,128)}, u32[]{:S(2)}) copy-start(f32[384,512]{1,0:T(8,128)} %get-tuple-element.67) | copy-start | bytes 2359300
  91.3 2.2 %copy-start.5 = (f32[384,512]{1,0:T(8,128)S(1)}, f32[384,512]{1,0:T(8,128)}, u32[]{:S(2)}) copy-start(f32[384,512]{1,0:T(8,128)} %get-tuple-element.69) | copy-start | bytes 2359300
  91.3 2.4 %copy-start.6 = (f32[384,512]{1,0:T(8,128)S(1)}, f32[384,512]{1,0:T(8,128)}, u32[]{:S(2)}) copy-start(f32[384,512]{1,0:T(8,128)} %get-tuple-element.71) | copy-start | bytes 2359300
  129.5 4.4 %copy-start.3 = (f32[384,512]{1,0:T(8,128)S(1)}, f32[384,512]{1,0:T(8,128)}, u32[]{:S(2)}) copy-start(f32[384,512]{1,0:T(8,128)} %get-tuple-element.67) | copy-start | bytes 2359300
Sparse Core Ops, SparseCore 0:
  143.7 48.6 reduce-scatter.3
where the time goes:
time: 206 us
  blocking collectives  99.4 us (48%)
  waiting for transfers between devices  48.8 us (24%)
  other arithmetic  19.9 us (10%)
  between operations  14.5 us (7%)
  matrix products  11.9 us (6%)
  local copies, waits for them, and re-layouts  11.1 us (5%)
    psum x3, blocking collectives, list_mass(): return lax.psum(partial_value, 'pts')  67.2 us
    unnamed x2, waiting for transfers between devices  48.8 us
    psum x3, blocking collectives, point_mass(): return lax.psum(partial_value, 'lists')  32.2 us
    unnamed x44, local copies, waits for them, and re-layouts  11.1 us
    dot_general x8, matrix products, kernel_tile(): lax.dot_general(points, cent_block, (((1,), (1,)), ((), ())), preferred_e...  8.58 us
    reduce_sum x3, other arithmetic, local(): jnp.sum(tile(index) * row_scale[:, None], axis=0)  8.21 us
    reduce_sum x12, other arithmetic, local(): jnp.sum(tile(index) * col_scale[None, index * BLOCK:(index + 1) * BLOCK],...  4.74 us
    unnamed x10, other arithmetic  4.33 us
  transfers between devices with their start and end apart: 1, of which 1 were waited for; matrix products, arithmetic and copies ran while one was open for 0% of the time, Pallas kernels for 0%

commit v1 on v0

v1 whole, which is shorter than its diff:
```python
import functools

import jax
import jax.numpy as jnp
from jax import lax
from jax.experimental import pallas as pl
from jax.experimental.pallas import tpu as pltpu

from jax.sharding import PartitionSpec as P

ITERS = 3
BLOCK = 512
LANES = 128
MESH = pl.DeviceIdType.MESH
NT = (((1,), (1,)), ((), ()))


def spread(row):
    return jnp.broadcast_to(row, (LANES, LANES)).T


def gather_up(block):
    return jnp.sum(block.T, axis=0, keepdims=True)


def kernel(
    n,
    nl,
    scale,
    pts_ref,
    cent_ref,
    prior_ref,
    loads_ref,
    out_ref,
    log_ref,
    mass,
    mass_t,
    allp,
    pts_t,
    plan_t,
    near,
    rowb,
    rowacc,
    col,
    row_out,
    row_in,
    col_out,
    col_in,
    row_all,
    sums,
    log_all,
    row_send,
    row_recv,
    col_send,
    col_recv,
    ag_send,
    ag_recv,
    fw_send,
    fw_recv,
    ra_send,
    ra_recv,
    out_send,
    out_recv,
    log_send,
    log_recv,
):
    p = lax.axis_index("pts")
    z = lax.axis_index("lists")
    m = pts_ref.shape[0]
    lists = cent_ref.shape[0]
    tiles = lists // LANES
    chunks = m // LANES
    share = lists // n
    share_tiles = share // LANES
    half = n // 2
    sibling = p + 1 - 2 * lax.rem(p, 2)

    def pt(k):
        return lax.rem(p + k, n)

    barrier = pltpu.get_barrier_semaphore()
    for k in range(1, n):
        pl.semaphore_signal(barrier, inc=1, device_id={"pts": pt(k)}, device_id_type=MESH)
    for k in range(1, nl):
        pl.semaphore_signal(
            barrier, inc=1, device_id={"lists": lax.rem(z + k, nl)}, device_id_type=MESH
        )

    allp[p, :m, :] = pts_ref[...].astype(jnp.float32)
    allp[p, m:, :] = jnp.zeros((8, allp.shape[2]), jnp.float32)
    row_out[...] = jnp.zeros_like(row_out)
    log_all[p] = jnp.zeros(log_all.shape[1:], jnp.float32)
    for r in range(chunks):
        prior_row = prior_ref[r : r + 1, :].astype(jnp.float32)
        allp[p, m + r : m + r + 1, 0:LANES] = prior_row
        near[r * LANES : (r + 1) * LANES, :] = spread(prior_row - (z * lists).astype(jnp.float32))
    pl.semaphore_wait(barrier, n - 1 + nl - 1)

    def remote(src, dst, send, recv, where):
        copy = pltpu.make_async_remote_copy(
            src_ref=src, dst_ref=dst, send_sem=send, recv_sem=recv,
            device_id=where, device_id_type=MESH,
        )
        copy.start()
        return copy

    started = []
    gathers = [remote(allp.at[p], allp.at[p], ag_send.at[0], ag_recv.at[0], {"pts": sibling})]
    for k in range(1, half):
        gathers.append(
            remote(allp.at[p], allp.at[p], ag_send.at[k], ag_recv.at[k], {"pts": pt(2 * k)})
        )
    started += gathers

    rowacc[...] = jnp.zeros_like(rowacc)
    per = BLOCK // LANES
    lane = lax.broadcasted_iota(jnp.int32, (m, LANES), 1).astype(jnp.float32)

    def make(b, carry):
        score = lax.dot_general(
            pts_ref[...], cent_ref[pl.ds(pl.multiple_of(b * BLOCK, BLOCK), BLOCK), :], NT,
            preferred_element_type=jnp.float32,
        )
        rel = near[...] - (b * BLOCK).astype(jnp.float32)
        total = rowacc[...]
        for c in range(per):
            hit = jnp.where(rel == lane + float(c * LANES), 10.0, 0.0)
            value = jnp.exp(3.0 * score[:, c * LANES : (c + 1) * LANES] + hit)
            mass[b * per + c] = value
            total = total + value
        rowacc[...] = total
        return carry

    lax.fori_loop(0, lists // BLOCK, make, 0)

    def send_rows(step):
        for r in range(chunks):
            row_out[step, r : r + 1, :] = gather_up(rowacc[r * LANES : (r + 1) * LANES, :])
        copies = [
            remote(
                row_out.at[step], row_in.at[step, k], row_send.at[step, k], row_recv.at[step, k],
                {"lists": lax.rem(z + k, nl)},
            )
            for k in range(1, nl)
        ]
        started.extend(copies)
        return copies

    def take_rows(step, copies):
        total = row_out[step]
        for k, copy in enumerate(copies, 1):
            copy.wait_recv()
            total = total + row_in[step, k]
        return 1.0 / total

    def send_cols(step, row):
        for r in range(chunks):
            rowb[r * LANES : (r + 1) * LANES, :] = spread(row[r : r + 1, :])

        def add(t, carry):
            col_out[step, pl.ds(t, 1), :] = jnp.sum(mass[t] * rowb[...], axis=0, keepdims=True)
            return carry

        lax.fori_loop(0, tiles, add, 0, unroll=4)
        copies = [
            remote(
                col_out.at[step], col_in.at[step, k], col_send.at[step, k], col_recv.at[step, k],
                {"pts": pt(k)},
            )
            for k in range(1, n)
        ]
        started.extend(copies)
        return copies

    def take_cols(step, copies):
        total = col_out[step]
        for k, copy in enumerate(copies, 1):
            copy.wait_recv()
            total = total + col_in[step, k]
        col[...] = loads_ref[...].astype(jnp.float32) * scale / total

    def add_rows():
        for r in range(chunks):
            part = pl.ds(r * LANES, LANES)

            def add(t, acc):
                return acc + mass[t, part, :] * col[pl.ds(t, 1), :]

            rowacc[part, :] = lax.fori_loop(
                0, tiles, add, jnp.zeros((LANES, LANES), jnp.float32), unroll=4
            )

    own = pl.multiple_of(p * share, share)
    first = (z * lists + p * share).astype(jnp.float32)
    index = lax.broadcasted_iota(jnp.int32, (share, LANES), 0).astype(jnp.float32) + first

    def part_of(s):
        piece = allp[s, :m, :]
        pts_t[:, pl.ds(pl.multiple_of(s * m, LANES), m)] = piece.T.astype(jnp.bfloat16)
        score = lax.dot_general(
            cent_ref[pl.ds(own, share), :], piece.astype(jnp.bfloat16), NT,
            preferred_element_type=jnp.float32,
        )
        for r in range(chunks):
            hit = jnp.where(index == allp[s, m + r : m + r + 1, 0:LANES], 10.0, 0.0)
            mass_t[s * chunks + r] = jnp.exp(3.0 * score[:, r * LANES : (r + 1) * LANES] + hit)

    copies = send_rows(0)
    part_of(p)
    row = take_rows(0, copies)
    copies = send_cols(0, row)
    gathers[0].wait_recv()
    part_of(sibling)
    take_cols(0, copies)
    add_rows()
    row = take_rows(1, send_rows(1))
    take_cols(1, send_cols(1, row))
    add_rows()
    copies = send_rows(2)
    forwards = []
    for k in range(1, half):
        gathers[k].wait_recv()
        source = pt(n - 2 * k)
        forwards.append(
            remote(
                allp.at[source], allp.at[source], fw_send.at[k], fw_recv.at[k], {"pts": sibling}
            )
        )
    started += forwards
    row_all[p] = take_rows(2, copies)
    copies = [
        remote(row_all.at[p], row_all.at[p], ra_send.at[k], ra_recv.at[k], {"pts": pt(k)})
        for k in range(1, n)
    ]
    started += copies

    def direct(k, carry):
        part_of(lax.rem(p + n - 2 * k, n))
        return carry

    lax.fori_loop(1, half, direct, 0)
    for copy in forwards:
        copy.wait_recv()

    def relayed(k, carry):
        part_of(lax.rem(sibling + n - 2 * k, n))
        return carry

    lax.fori_loop(1, half, relayed, 0)
    for copy in copies:
        copy.wait_recv()

    for c in range(share_tiles):
        part = pl.ds(c * LANES, LANES)

        def add(s, acc):
            for r in range(chunks):
                acc = acc + mass_t[s * chunks + r, part, :] * row_all[s, r : r + 1, :]
            return acc

        acc = lax.fori_loop(0, n, add, jnp.zeros((LANES, LANES), jnp.float32))
        total = jnp.sum(acc, axis=1, keepdims=True)
        target = loads_ref[pl.ds(p * share_tiles + c, 1), :].astype(jnp.float32) * scale
        colb = spread(target) / total
        log_all[p, c : c + 1, :] = jnp.log(colb).T[0:1, :]

        def plan(s, carry):
            for r in range(chunks):
                value = mass_t[s * chunks + r, part, :] * row_all[s, r : r + 1, :] * colb
                plan_t[part, pl.ds(pl.multiple_of(s * m + r * LANES, LANES), LANES)] = value.astype(
                    jnp.bfloat16
                )
            return carry

        lax.fori_loop(0, n, plan, 0)
    copies = [
        remote(log_all.at[p], log_all.at[p], log_send.at[k], log_recv.at[k], {"pts": pt(k)})
        for k in range(1, n)
    ]
    total = lax.dot_general(pts_t[...], plan_t[...], NT, preferred_element_type=jnp.float32)
    depth = out_ref.shape[0]
    for c in range(share_tiles):
        target = loads_ref[pl.ds(p * share_tiles + c, 1), :].astype(jnp.float32) * scale
        part = total[:, c * LANES : (c + 1) * LANES] / target
        for q in range(n):
            sums[q, :, c * LANES : (c + 1) * LANES] = part[q * depth : (q + 1) * depth, :]
    copies += [
        remote(
            sums.at[pt(k)], out_ref.at[:, pl.ds(own, share)], out_send.at[k], out_recv.at[k],
            {"pts": pt(k)},
        )
        for k in range(1, n)
    ]
    out_ref[:, pl.ds(own, share)] = sums[p]
    for copy in copies:
        copy.wait_recv()
    for s in range(n):
        log_ref[s * share_tiles : (s + 1) * share_tiles, :] = log_all[s, :share_tiles, :]
    for copy in started + copies:
        copy.wait_send()


def local(n, nl, points, centroids, prior, loads):
    m, dim = points.shape
    lists = centroids.shape[0]
    tiles = lists // LANES
    chunks = m // LANES
    share = lists // n
    scale = (m * n) / (8.0 * lists * nl)
    f32 = jnp.float32
    dma = pltpu.SemaphoreType.DMA
    out, log = pl.pallas_call(
        functools.partial(kernel, n, nl, scale),
        out_shape=(
            jax.ShapeDtypeStruct((dim // n, lists), f32),
            jax.ShapeDtypeStruct((tiles, LANES), f32),
        ),
        in_specs=[pl.BlockSpec(memory_space=pltpu.VMEM)] * 4,
        out_specs=[pl.BlockSpec(memory_space=pltpu.VMEM)] * 2,
        scratch_shapes=[
            pltpu.VMEM((tiles, m, LANES), f32),
            pltpu.VMEM((n * chunks, share, LANES), f32),
            pltpu.VMEM((n, m + 8, dim), f32),
            pltpu.VMEM((dim, n * m), jnp.bfloat16),
            pltpu.VMEM((share, n * m), jnp.bfloat16),
            pltpu.VMEM((m, LANES), f32),
            pltpu.VMEM((m, LANES), f32),
            pltpu.VMEM((m, LANES), f32),
            pltpu.VMEM((tiles, LANES), f32),
            pltpu.VMEM((ITERS, 8, LANES), f32),
            pltpu.VMEM((ITERS, nl, 8, LANES), f32),
            pltpu.VMEM((ITERS - 1, tiles, LANES), f32),
            pltpu.VMEM((ITERS - 1, n, tiles, LANES), f32),
            pltpu.VMEM((n, 8, LANES), f32),
            pltpu.VMEM((n, dim // n, share), f32),
            pltpu.VMEM((n, 8, LANES), f32),
            dma((ITERS, nl)),
            dma((ITERS, nl)),
            dma((ITERS - 1, n)),
            dma((ITERS - 1, n)),
            dma((n // 2,)),
            dma((n // 2,)),
            dma((n // 2,)),
            dma((n // 2,)),
            dma((n,)),
            dma((n,)),
            dma((n,)),
            dma((n,)),
            dma((n,)),
            dma((n,)),
        ],
        compiler_params=pltpu.CompilerParams(
            collective_id=0, has_side_effects=True, vmem_limit_bytes=56 * 1024 * 1024
        ),
    )(points, centroids, prior.reshape(chunks, LANES), loads.reshape(tiles, LANES))
    return out, log.reshape(lists)


def solution(mesh):
    return jax.shard_map(
        functools.partial(local, mesh.shape["pts"], mesh.shape["lists"]),
        mesh=mesh,
        in_specs=(P("pts", None), P("lists", None), P("pts"), P("lists")),
        out_specs=(P("pts", "lists"), P("lists")),
        check_vma=False,
    )
```

time: 206 us -> 60 us (0.29)
  blocking collectives: 99.4 us -> 0 us
  Pallas kernels: 0 us -> 55.5 us
  waiting for transfers between devices: 48.8 us -> 0 us
  other arithmetic: 19.9 us -> 0 us
  between operations: 14.5 us -> 0.64 us
  matrix products: 11.9 us -> 0 us
  local copies, waits for them, and re-layouts: 11.1 us -> 3.19 us
    psum x6 -> x0, blocking collectives: 99.4 us -> none  [the longest x3 67.2 us: list_mass(): return lax.psum(partial_value, 'pts')]
    pallas_call x0 -> x1, Pallas kernels: none -> 55.5 us  [local(): pl.pallas_call(functools.partial(kernel, n, nl, scale), out_shape=(jax.Sh...]
    unnamed x2 -> x0, waiting for transfers between devices: 48.8 us -> none
    reduce_sum x15 -> x0, other arithmetic: 13 us -> none  [the longest x3 8.21 us: local(): jnp.sum(tile(index) * row_scale[:, None], axis=0)]
    dot_general x9 -> x0, matrix products: 11.9 us -> none  [the longest x8 8.58 us: kernel_tile(): lax.dot_general(points, cent_block, (((1,), (1,)), ((), ())), preferred_e...]
    unnamed x44 -> x2, local copies, waits for them, and re-layouts: 11.1 us -> 3.19 us
    unnamed x10 -> x0, other arithmetic: 4.33 us -> none
  transfers between devices with their start and end apart: 1 -> 0, of which waited for: 1 -> 0; matrix products, arithmetic and copies ran while one was open for 0% -> 0% of each run, Pallas kernels for 0% -> 0%
where the time goes in v1:
time: 60 us; the launch traced here: 59.3 us
  Pallas kernels  55.5 us (92%)
  local copies, waits for them, and re-layouts  3.19 us (5%)
  between operations  0.64 us (1%)
    pallas_call x1, Pallas kernels, local(): pl.pallas_call(functools.partial(kernel, n, nl, scale), out_shape=(jax.Sh...  55.5 us
    unnamed x2, local copies, waits for them, and re-layouts  3.19 us

profile of v1, /device:TPU:0, one launch (start us, length us, event | category | flops | bytes accessed | tf_op | source)
XLA Modules:
  0.0 59.3 jit_solution(16112908349124702788)
XLA Ops:
  0.6 55.5 %shard_map.59 = (f32[32,4096]{1,0:T(8,128)}, f32[32,128]{1,0:T(8,128)}) custom-call(bf16[384,256]{1,0:T(8,128)(2,1)} %pts_ref.1, bf16[4096,256]{1,0:T(8,128)(2,1)} %cent_ref.1, s32[3,128]{1,0:T(4,128)} %bitcast.5, s32[32,128]{1,0:T(8,128)} %bitcast.3), custom_call_target="tpu_custom_call" | custom-call | tf_op jit(solution)/shard_map/pallas_call | solution.py:312
  56.1 1.9 %copy.8 = f32[32,4096]{1,0:T(8,128)} copy(f32[32,4096]{1,0:T(8,128)} %get-tuple-element.8) | data formatting | bytes 1048576
  58.0 1.3 %copy.9 = f32[4096]{0:T(1024)} copy(f32[4096]{0:T(1024)} %bitcast.4) | data formatting | bytes 32768

commit v2 on v1

--- a/solution.py
+++ b/solution.py
@@ -27,8 +27,10 @@
     n,
     nl,
     scale,
+    paced,
+    group,
     pts_ref,
-    cent_ref,
+    cent_hbm,
     prior_ref,
     loads_ref,
     out_ref,
@@ -63,6 +65,8 @@
     out_recv,
     log_send,
     log_recv,
+    cent_ref,
+    cent_sem,
 ):
     p = lax.axis_index("pts")
     z = lax.axis_index("lists")
@@ -78,6 +82,8 @@
     def pt(k):
         return lax.rem(p + k, n)
 
+    fetch = pltpu.make_async_copy(cent_hbm, cent_ref, cent_sem)
+    fetch.start()
     barrier = pltpu.get_barrier_semaphore()
     for k in range(1, n):
         pl.semaphore_signal(barrier, inc=1, device_id={"pts": pt(k)}, device_id_type=MESH)
@@ -105,12 +111,27 @@
         return copy
 
     started = []
-    gathers = [remote(allp.at[p], allp.at[p], ag_send.at[0], ag_recv.at[0], {"pts": sibling})]
-    for k in range(1, half):
-        gathers.append(
-            remote(allp.at[p], allp.at[p], ag_send.at[k], ag_recv.at[k], {"pts": pt(2 * k)})
-        )
-    started += gathers
+
+    def send_piece(source, rows, send, recv, where):
+        copy = remote(allp.at[source, rows], allp.at[source, rows], send, recv, {"pts": where})
+        started.append(copy)
+        return copy
+
+    whole = pl.ds(0, m + 8)
+    near_sib = send_piece(p, whole, ag_send.at[0], ag_recv.at[0], sibling)
+    if paced:
+        over_x = p + 2 - 4 * lax.rem(p // 2, 2)
+        over_y = p + 4 - 8 * lax.rem(p // 4, 2)
+        across = over_x + 4 - 8 * lax.rem(p // 4, 2)
+        first_rows, last_rows = pl.ds(0, m // 2), pl.ds(m // 2, m // 2 + 8)
+        head = [
+            send_piece(p, first_rows, ag_send.at[1], ag_recv.at[1], over_x),
+            send_piece(p, first_rows, ag_send.at[2], ag_recv.at[2], over_y),
+        ]
+    else:
+        gathers = [
+            send_piece(p, whole, ag_send.at[k], ag_recv.at[k], pt(2 * k)) for k in range(1, half)
+        ]
 
     rowacc[...] = jnp.zeros_like(rowacc)
     per = BLOCK // LANES
@@ -131,6 +152,7 @@
         rowacc[...] = total
         return carry
 
+    fetch.wait()
     lax.fori_loop(0, lists // BLOCK, make, 0)
 
     def send_rows(step):
@@ -209,95 +231,156 @@
     part_of(p)
     row = take_rows(0, copies)
     copies = send_cols(0, row)
-    gathers[0].wait_recv()
+    near_sib.wait_recv()
     part_of(sibling)
     take_cols(0, copies)
+    if paced:
+        tail = [
+            send_piece(p, last_rows, ag_send.at[3], ag_recv.at[3], over_x),
+            send_piece(p, last_rows, ag_send.at[4], ag_recv.at[4], over_y),
+        ]
     add_rows()
     row = take_rows(1, send_rows(1))
     take_cols(1, send_cols(1, row))
+    if paced:
+        for copy in head + tail:
+            copy.wait_recv()
+        on = [
+            send_piece(over_x, first_rows, ag_send.at[5], ag_recv.at[5], over_y),
+            send_piece(over_y, last_rows, ag_send.at[6], ag_recv.at[6], over_x),
+        ]
+        forwards = [
+            send_piece(over_x, whole, fw_send.at[1], fw_recv.at[1], sibling),
+            send_piece(over_y, whole, fw_send.at[2], fw_recv.at[2], sibling),
+        ]
     add_rows()
     copies = send_rows(2)
-    forwards = []
-    for k in range(1, half):
-        gathers[k].wait_recv()
-        source = pt(n - 2 * k)
-        forwards.append(
-            remote(
-                allp.at[source], allp.at[source], fw_send.at[k], fw_recv.at[k], {"pts": sibling}
-            )
-        )
-    started += forwards
+    if not paced:
+        forwards = []
+        for k in range(1, half):
+            gathers[k - 1].wait_recv()
+            source = pt(n - 2 * k)
+            forwards.append(send_piece(source, whole, fw_send.at[k], fw_recv.at[k], sibling))
     row_all[p] = take_rows(2, copies)
     copies = [
         remote(row_all.at[p], row_all.at[p], ra_send.at[k], ra_recv.at[k], {"pts": pt(k)})
         for k in range(1, n)
     ]
     started += copies
-
-    def direct(k, carry):
-        part_of(lax.rem(p + n - 2 * k, n))
-        return carry
-
-    lax.fori_loop(1, half, direct, 0)
-    for copy in forwards:
-        copy.wait_recv()
-
-    def relayed(k, carry):
-        part_of(lax.rem(sibling + n - 2 * k, n))
-        return carry
-
-    lax.fori_loop(1, half, relayed, 0)
+    if paced:
+
+        def pair(first, second):
+            def one(k, carry):
+                part_of(first + k * (second - first))
+                return carry
+
+            lax.fori_loop(0, 2, one, 0)
+
+        pair(over_x, over_y)
+        for copy in on:
+            copy.wait_recv()
+        forwards.append(send_piece(across, whole, fw_send.at[3], fw_recv.at[3], sibling))
+        for copy in forwards[:2]:
+            copy.wait_recv()
+        across_sib = across + 1 - 2 * lax.rem(p, 2)
+        pair(over_x + sibling - p, over_y + sibling - p)
+        part_of(across)
+        forwards[2].wait_recv()
+        part_of(across_sib)
+    else:
+
+        def direct(k, carry):
+            part_of(lax.rem(p + n - 2 * k, n))
+            return carry
+
+        lax.fori_loop(1, half, direct, 0)
+        for copy in forwards:
+            copy.wait_recv()
+
+        def relayed(k, carry):
+            part_of(lax.rem(sibling + n - 2 * k, n))
+            return carry
+
+        lax.fori_loop(1, half, relayed, 0)
     for copy in copies:
         copy.wait_recv()
 
-    for c in range(share_tiles):
-        part = pl.ds(c * LANES, LANES)
-
-        def add(s, acc):
-            for r in range(chunks):
-                acc = acc + mass_t[s * chunks + r, part, :] * row_all[s, r : r + 1, :]
-            return acc
-
-        acc = lax.fori_loop(0, n, add, jnp.zeros((LANES, LANES), jnp.float32))
-        total = jnp.sum(acc, axis=1, keepdims=True)
-        target = loads_ref[pl.ds(p * share_tiles + c, 1), :].astype(jnp.float32) * scale
-        colb = spread(target) / total
-        log_all[p, c : c + 1, :] = jnp.log(colb).T[0:1, :]
-
-        def plan(s, carry):
-            for r in range(chunks):
-                value = mass_t[s * chunks + r, part, :] * row_all[s, r : r + 1, :] * colb
-                plan_t[part, pl.ds(pl.multiple_of(s * m + r * LANES, LANES), LANES)] = value.astype(
-                    jnp.bfloat16
+    depth = out_ref.shape[0]
+    order = [k for k in range(1, n)][::-1]
+    copies = []
+
+    def finish(g):
+        width = group * LANES
+        for c in range(g * group, (g + 1) * group):
+            part = pl.ds(c * LANES, LANES)
+
+            def add(s, acc):
+                for r in range(chunks):
+                    acc = acc + mass_t[s * chunks + r, part, :] * row_all[s, r : r + 1, :]
+                return acc
+
+            acc = lax.fori_loop(0, n, add, jnp.zeros((LANES, LANES), jnp.float32), unroll=2)
+            total = jnp.sum(acc, axis=1, keepdims=True)
+            target = loads_ref[pl.ds(p * share_tiles + c, 1), :].astype(jnp.float32) * scale
+            colb = spread(target) / total
+            log_all[p, c : c + 1, :] = jnp.log(colb).T[0:1, :]
+
+            def plan(s, carry):
+                for r in range(chunks):
+                    value = mass_t[s * chunks + r, part, :] * row_all[s, r : r + 1, :] * colb
+                    spot = pl.ds(pl.multiple_of(s * m + r * LANES, LANES), LANES)
+                    plan_t[part, spot] = value.astype(jnp.bfloat16)
+                return carry
+
+            lax.fori_loop(0, n, plan, 0, unroll=2)
+        total = lax.dot_general(
+            pts_t[...], plan_t[g * width : (g + 1) * width, :], NT,
+            preferred_element_type=jnp.float32,
+        )
+        for c in range(group):
+            target = loads_ref[
+                pl.ds(p * share_tiles + g * group + c, 1), :
+            ].astype(jnp.float32) * scale
+            part = total[:, c * LANES : (c + 1) * LANES] * (1.0 / target)
+            for q in range(n):
+                sums[g, q, :, c * LANES : (c + 1) * LANES] = part[q * depth : (q + 1) * depth, :]
+        spot = pl.ds(pl.multiple_of(p * share + g * width, LANES), width)
+        for k in order:
+            copies.append(
+                remote(
+                    sums.at[g, pt(k)], out_ref.at[:, spot], out_send.at[g, k], out_recv.at[g, k],
+                    {"pts": pt(k)},
                 )
-            return carry
-
-        lax.fori_loop(0, n, plan, 0)
-    copies = [
+            )
+        out_ref[:, spot] = sums[g, p]
+
+    for g in range(share_tiles // group):
+        finish(g)
+    copies += [
         remote(log_all.at[p], log_all.at[p], log_send.at[k], log_recv.at[k], {"pts": pt(k)})
-        for k in range(1, n)
+        for k in order
     ]
-    total = lax.dot_general(pts_t[...], plan_t[...], NT, preferred_element_type=jnp.float32)
-    depth = out_ref.shape[0]
-    for c in range(share_tiles):
-        target = loads_ref[pl.ds(p * share_tiles + c, 1), :].astype(jnp.float32) * scale
-        part = total[:, c * LANES : (c + 1) * LANES] / target
-        for q in range(n):
-            sums[q, :, c * LANES : (c + 1) * LANES] = part[q * depth : (q + 1) * depth, :]
-    copies += [
-        remote(
-            sums.at[pt(k)], out_ref.at[:, pl.ds(own, share)], out_send.at[k], out_recv.at[k],
-            {"pts": pt(k)},
-        )
-        for k in range(1, n)
-    ]
-    out_ref[:, pl.ds(own, share)] = sums[p]
     for copy in copies:
         copy.wait_recv()
     for s in range(n):
         log_ref[s * share_tiles : (s + 1) * share_tiles, :] = log_all[s, :share_tiles, :]
     for copy in started + copies:
         copy.wait_send()
+
+
+def hand_on(out_in, log_in, out_ref, log_ref, sem):
+    rows = out_in.shape[0] // 8
+    copies = [
+        pltpu.make_async_copy(
+            out_in.at[8 * i : 8 * i + 8], out_ref.at[8 * i : 8 * i + 8], sem.at[i]
+        )
+        for i in range(rows)
+    ]
+    copies.append(pltpu.make_async_copy(log_in, log_ref, sem.at[rows]))
+    for copy in copies:
+        copy.start()
+    for copy in copies:
+        copy.wait()
 
 
 def local(n, nl, points, centroids, prior, loads):
@@ -307,15 +390,22 @@
     chunks = m // LANES
     share = lists // n
     scale = (m * n) / (8.0 * lists * nl)
+    paced = n == 8
+    group = min(2, share // LANES)
     f32 = jnp.float32
     dma = pltpu.SemaphoreType.DMA
     out, log = pl.pallas_call(
-        functools.partial(kernel, n, nl, scale),
+        functools.partial(kernel, n, nl, scale, paced, group),
         out_shape=(
             jax.ShapeDtypeStruct((dim // n, lists), f32),
             jax.ShapeDtypeStruct((tiles, LANES), f32),
         ),
-        in_specs=[pl.BlockSpec(memory_space=pltpu.VMEM)] * 4,
+        in_specs=[
+            pl.BlockSpec(memory_space=pltpu.VMEM),
+            pl.BlockSpec(memory_space=pl.ANY),
+            pl.BlockSpec(memory_space=pltpu.VMEM),
+            pl.BlockSpec(memory_space=pltpu.VMEM),
+        ],
         out_specs=[pl.BlockSpec(memory_space=pltpu.VMEM)] * 2,
         scratch_shapes=[
             pltpu.VMEM((tiles, m, LANES), f32),
@@ -332,27 +422,39 @@
             pltpu.VMEM((ITERS - 1, tiles, LANES), f32),
             pltpu.VMEM((ITERS - 1, n, tiles, LANES), f32),
             pltpu.VMEM((n, 8, LANES), f32),
-            pltpu.VMEM((n, dim // n, share), f32),
+            pltpu.VMEM((share // LANES // group, n, dim // n, group * LANES), f32),
             pltpu.VMEM((n, 8, LANES), f32),
             dma((ITERS, nl)),
             dma((ITERS, nl)),
             dma((ITERS - 1, n)),
             dma((ITERS - 1, n)),
-            dma((n // 2,)),
-            dma((n // 2,)),
+            dma((max(n // 2, 7),)),
+            dma((max(n // 2, 7),)),
             dma((n // 2,)),
             dma((n // 2,)),
             dma((n,)),
             dma((n,)),
+            dma((share // LANES // group, n)),
+            dma((share // LANES // group, n)),
             dma((n,)),
             dma((n,)),
-            dma((n,)),
-            dma((n,)),
+            pltpu.VMEM((lists, dim), jnp.bfloat16),
+            dma,
         ],
         compiler_params=pltpu.CompilerParams(
             collective_id=0, has_side_effects=True, vmem_limit_bytes=56 * 1024 * 1024
         ),
     )(points, centroids, prior.reshape(chunks, LANES), loads.reshape(tiles, LANES))
+    out, log = pl.pallas_call(
+        hand_on,
+        out_shape=(
+            jax.ShapeDtypeStruct(out.shape, f32),
+            jax.ShapeDtypeStruct(log.shape, f32),
+        ),
+        in_specs=[pl.BlockSpec(memory_space=pl.ANY)] * 2,
+        out_specs=[pl.BlockSpec(memory_space=pl.ANY)] * 2,
+        scratch_shapes=[dma((dim // n // 8 + 1,))],
+    )(out, log)
     return out, log.reshape(lists)
 
 

time: 60 us -> 65.9 us (1.098)
  Pallas kernels: 55.5 us -> 65.1 us
  local copies, waits for them, and re-layouts: 3.19 us -> 0 us
    pallas_call x1 -> x2, Pallas kernels: 55.5 us -> 65.1 us  [the longest x1 47.6 us: local(): pl.pallas_call(functools.partial(kernel, n, nl, scale, paced, group), out...]
    unnamed x2 -> x0, local copies, waits for them, and re-layouts: 3.19 us -> none
where the time goes in v2:
time: 65.9 us; the launch traced here: 65.8 us
  Pallas kernels  65.1 us (99%)
    pallas_call x1, Pallas kernels, local(): pl.pallas_call(functools.partial(kernel, n, nl, scale, paced, group), out...  47.6 us
    pallas_call x1, Pallas kernels, local(): pl.pallas_call(hand_on, out_shape=(jax.ShapeDtypeStruct(out.shape, f32),...  17.5 us

profile of v2, /device:TPU:0, one launch (start us, length us, event | category | flops | bytes accessed | tf_op | source)
XLA Modules:
  0.0 65.8 jit_solution(18254490594823045523)
XLA Ops:
  0.6 47.6 %shard_map.59 = (f32[32,4096]{1,0:T(8,128)}, f32[32,128]{1,0:T(8,128)}) custom-call(bf16[384,256]{1,0:T(8,128)(2,1)} %pts_ref.1, bf16[4096,256]{1,0:T(8,128)(2,1)} %cent_hbm.1, s32[3,128]{1,0:T(4,128)} %bitcast.4, s32[32,128]{1,0:T(8,128)} %bitcast.3), custom_call_target="tpu_custom_call" | custom-call | tf_op jit(solution)/shard_map/pallas_call | solution.py:397
  48.2 17.5 %shard_map.60 = (f32[32,4096]{1,0:T(8,128)}, f32[32,128]{1,0:T(8,128)}) custom-call(f32[32,4096]{1,0:T(8,128)} %get-tuple-element.6.out_in, f32[32,128]{1,0:T(8,128)} %get-tuple-element.7.log_in), custom_call_target="tpu_custom_call" | custom-call | tf_op jit(solution)/shard_map/pallas_call | solution.py:448

commit v3 on v2

--- a/solution.py
+++ b/solution.py
@@ -368,18 +368,20 @@
         copy.wait_send()
 
 
-def hand_on(out_in, log_in, out_ref, log_ref, sem):
-    rows = out_in.shape[0] // 8
-    copies = [
-        pltpu.make_async_copy(
-            out_in.at[8 * i : 8 * i + 8], out_ref.at[8 * i : 8 * i + 8], sem.at[i]
-        )
-        for i in range(rows)
-    ]
-    copies.append(pltpu.make_async_copy(log_in, log_ref, sem.at[rows]))
-    for copy in copies:
+def hand_on(out_in, log_in, out_ref, log_ref, out_held, log_held, in_sem, out_sem):
+    rows = [pl.ds(8 * i, 8) for i in range(out_in.shape[0] // 8)]
+    stages = [(out_in.at[r], out_held.at[r], out_ref.at[r]) for r in rows]
+    stages.append((log_in, log_held, log_ref))
+    fetches, stores = [], []
+    for i, (source, held, dest) in enumerate(stages):
+        fetches.append(pltpu.make_async_copy(source, held, in_sem.at[i]))
+        stores.append(pltpu.make_async_copy(held, dest, out_sem.at[i]))
+    for copy in fetches:
         copy.start()
-    for copy in copies:
+    for fetch, store in zip(fetches, stores):
+        fetch.wait()
+        store.start()
+    for copy in stores:
         copy.wait()
 
 
@@ -453,7 +455,12 @@
         ),
         in_specs=[pl.BlockSpec(memory_space=pl.ANY)] * 2,
         out_specs=[pl.BlockSpec(memory_space=pl.ANY)] * 2,
-        scratch_shapes=[dma((dim // n // 8 + 1,))],
+        scratch_shapes=[
+            pltpu.VMEM(out.shape, f32),
+            pltpu.VMEM(log.shape, f32),
+            dma((dim // n // 8 + 1,)),
+            dma((dim // n // 8 + 1,)),
+        ],
     )(out, log)
     return out, log.reshape(lists)
 

time: 65.9 us -> 50.2 us (0.76)
  Pallas kernels: 65.1 us -> 49.4 us
    pallas_call x1, Pallas kernels: 17.5 us -> 1.84 us  [local(): pl.pallas_call(hand_on, out_shape=(jax.ShapeDtypeStruct(out.shape, f32),...]
where the time goes in v3:
time: 50.2 us; the launch traced here: 50.1 us
  Pallas kernels  49.4 us (98%)
  between operations  0.64 us (1%)
    pallas_call x1, Pallas kernels, local(): pl.pallas_call(functools.partial(kernel, n, nl, scale, paced, group), out...  47.6 us
    pallas_call x1, Pallas kernels, local(): pl.pallas_call(hand_on, out_shape=(jax.ShapeDtypeStruct(out.shape, f32),...  1.84 us

profile of v3, /device:TPU:0, one launch (start us, length us, event | category | flops | bytes accessed | tf_op | source)
XLA Modules:
  0.0 50.1 jit_solution(144407237610451244)
XLA Ops:
  0.6 47.6 %shard_map.59 = (f32[32,4096]{1,0:T(8,128)}, f32[32,128]{1,0:T(8,128)}) custom-call(bf16[384,256]{1,0:T(8,128)(2,1)} %pts_ref.1, bf16[4096,256]{1,0:T(8,128)(2,1)} %cent_hbm.1, s32[3,128]{1,0:T(4,128)} %bitcast.4, s32[32,128]{1,0:T(8,128)} %bitcast.3), custom_call_target="tpu_custom_call" | custom-call | tf_op jit(solution)/shard_map/pallas_call | solution.py:399
  48.2 1.8 %shard_map.60 = (f32[32,4096]{1,0:T(8,128)}, f32[32,128]{1,0:T(8,128)}) custom-call(f32[32,4096]{1,0:T(8,128)} %get-tuple-element.6.out_in, f32[32,128]{1,0:T(8,128)} %get-tuple-element.7.log_in), custom_call_target="tpu_custom_call" | custom-call | tf_op jit(solution)/shard_map/pallas_call | solution.py:450
